TPU v7x, 512 devices: a whole 4x4x16 slice. The times are simulated.
512 devices in a mesh: segment: 8 (over y, core), expert: 64 (over x, z).
Axes of the slice: x: 4, y: 4, z: 16, core: 2. Of those that a mesh axis runs over, the one named last changes fastest.
Arguments:
- hidden: bfloat16 [8, 2048, 2048], P('segment', 'expert'), may hold values from -6 to 6
- memory: bfloat16 [8, 2048, 2048], P('segment', 'expert'), may hold values from -6 to 6
- lengths: int32 [8, 64], P('segment', 'expert'), may hold values from 1 to 32, as said below
- memory_lengths: int32 [8, 64], P('segment', 'expert'), may hold values from 1 to 32, as said below
- routes: int32 [8, 2048, 2], P('segment', 'expert'), may hold values from 0 to 3, all different within a row; in each aligned block of 32 rows (0 to 31, 32 to 63, ..., all dimensions but the last counted through in order) at most 20 rows name the same one
- norm_gain: float32 [8, 3, 2048], P('segment'), may hold values from 0.5 to 1.5, as said below
- router: bfloat16 [8, 2048, 4], P('segment'), may hold values from -0.26516504 to 0.26516504, as said below
- w_in: bfloat16 [8, 2048, 16384], P('segment', None, 'expert'), may hold values from -0.13258252 to 0.13258252, as said below
- w_out: bfloat16 [8, 16384, 2048], P('segment', 'expert'), may hold values from -0.125 to 0.125, as said below
- shortlist: bfloat16 [8, 2048, 512], P('segment'), may hold values from -0.375 to 0.375
- student: float32 [8, 2048, 512], P('segment', 'expert'), may hold values from -15 to 15
- targets: int32 [8, 2048], P('segment', 'expert'), may hold values from 0 to 511
Outputs:
- layer_out: bfloat16 [8, 2048, 2048], P('segment', 'expert')
- loss: float32 [], replicated
Inputs may be any that keep to these rules, and one draw needn't show every extreme that they name: `lengths`: every sequence has at least one position; the first sequence of each section has 32. `memory_lengths`: every sequence has at least one position; the first sequence of each section has 32. `routes`: A token's two experts differ. In the 32 rows of one device no expert is named more than 20 times, a bound that some block reaches. `norm_gain`: equal in all encoder sections, and equal in all decoder sections. `router`: equal in all encoder sections, and equal in all decoder sections. `w_in`: equal in all encoder sections, and equal in all decoder sections. `w_out`: equal in all encoder sections, and equal in all decoder sections.
All inputs are finite; a program needn't handle non-finite values.
Results may differ from a plain program's by a relative error of at most 0.0049.
Values may be sent and summed in bfloat16 or wider, within the bound.
No kernel may reach another device: no remote copies, remote signals or barrier semaphores. Data moves between devices by JAX's collectives and lax.ppermute only.
A program may use at most 64 MiB of HBM per device.

v0:
```python
import math
import jax
import jax.numpy as jnp
from jax import lax
from jax.sharding import Mesh, PartitionSpec as P

HEADS = 16
HEAD_DIM = 128
LEN = 32
epsilon = 1e-05


def passed_along(block, axis, distance):
    devices = range(lax.axis_size(axis))
    route = [(i - distance, i) for i in devices if i - distance in devices]
    return lax.ppermute(block, axis, route)


def layer_norm(values, gain_row):
    centred = values - jnp.mean(values, axis=-1, keepdims=True)
    spread = jnp.mean(centred * centred, axis=-1, keepdims=True)
    return centred * lax.rsqrt(spread + epsilon) * gain_row


def expert_rows(rows, first_weight, second_weight):
    activated = jnp.maximum(
        jnp.dot(rows, first_weight, preferred_element_type=jnp.float32), 0.0
    ).astype(jnp.bfloat16)
    return jnp.dot(activated, second_weight, preferred_element_type=jnp.float32).astype(
        jnp.bfloat16
    )


def local(
    hidden,
    memory,
    lengths,
    memory_lengths,
    routes,
    norm_gain,
    router,
    w_in,
    w_out,
    shortlist,
    student,
    targets,
):
    chips = lax.axis_size("y")
    experts = router.shape[2]
    tok_rows = hidden.shape[1]
    model_width = hidden.shape[2]
    capacity = 5 * tok_rows // 8
    decoder = lax.axis_index("y") >= chips // 2
    positions = jnp.arange(tok_rows) % LEN
    seq_index = jnp.arange(tok_rows) // LEN
    is_valid = positions < lengths[0][seq_index]
    key_mask = (positions < memory_lengths[0][seq_index]).astype(jnp.bfloat16)
    arrived, arrived_mask = passed_along((memory[0], key_mask), "y", chips // 2)
    states = hidden[0].astype(jnp.float32)
    gain_rows = norm_gain[0]
    seq_count = tok_rows // LEN
    score_scale = 1.0 / math.sqrt(HEAD_DIM)
    queries = (
        layer_norm(states, gain_rows[0])
        .astype(jnp.bfloat16)
        .reshape(seq_count, LEN, HEADS, HEAD_DIM)
    )
    key_rows = arrived.reshape(seq_count, LEN, HEADS, HEAD_DIM)
    scores = (
        jnp.einsum("bqhd,bkhd->bhqk", queries, key_rows, preferred_element_type=jnp.float32)
        * score_scale
    )
    allowed = arrived_mask.reshape(seq_count, 1, 1, LEN) > 0.5
    scores = jnp.where(allowed, scores, -1e30)
    weights = jax.nn.softmax(scores, axis=-1).astype(jnp.bfloat16)
    attended = jnp.einsum(
        "bhqk,bkhd->bqhd", weights, key_rows, preferred_element_type=jnp.float32
    ).reshape(tok_rows, model_width)
    mid_states = states + jnp.where(decoder, attended, 0.0)
    normed = layer_norm(mid_states, gain_rows[1]).astype(jnp.bfloat16)
    router_probs = jax.nn.softmax(
        jnp.dot(normed, router[0], preferred_element_type=jnp.float32), axis=-1
    )
    expert_ids = jnp.arange(experts)
    first_hot = (routes[0][:, 0:1] == expert_ids).astype(jnp.float32)
    second = (routes[0][:, 1:2] == expert_ids).astype(jnp.float32)
    prob_first = jnp.sum(router_probs * first_hot, axis=-1, keepdims=True)
    prob_second = jnp.sum(router_probs * second, axis=-1, keepdims=True)
    prob_total = prob_first + prob_second
    gate_rows = (prob_first * first_hot + prob_second * second) / prob_total
    chosen = (first_hot + second) * is_valid[:, None].astype(jnp.float32)
    upto = (jnp.arange(tok_rows)[:, None] >= jnp.arange(tok_rows)[None, :]).astype(jnp.float32)
    slot_rank = jnp.dot(upto, chosen, preferred_element_type=jnp.float32) - 1.0
    slot_ids = jnp.arange(capacity).astype(jnp.float32)
    placing = chosen.T[:, None, :] * (slot_rank.T[:, None, :] == slot_ids[None, :, None]).astype(
        jnp.float32
    )
    buffer = jnp.einsum(
        "ect,td->ecd", placing.astype(jnp.bfloat16), normed, preferred_element_type=jnp.float32
    ).astype(jnp.bfloat16)
    at_expert = lax.all_to_all(buffer, "x", split_axis=0, concat_axis=0, tiled=True)
    rows = lax.all_gather(
        at_expert.reshape(experts * capacity, model_width), "z", axis=0, tiled=True
    )
    partial_out = expert_rows(rows, w_in[0], w_out[0])
    expert_sum = lax.psum_scatter(partial_out, "z", scatter_dimension=0, tiled=True)
    summed = lax.all_to_all(
        expert_sum.reshape(experts, capacity, model_width),
        "x",
        split_axis=0,
        concat_axis=0,
        tiled=True,
    ).astype(jnp.float32)
    weighting = placing * gate_rows.T[:, None, :]
    moe_out = jnp.einsum("ect,ecd->td", weighting, summed, precision=lax.Precision.HIGHEST)
    layer_out = (mid_states + moe_out).astype(jnp.bfloat16)
    final_normed = layer_norm(layer_out.astype(jnp.float32), gain_rows[2]).astype(jnp.bfloat16)
    teacher = jax.nn.log_softmax(
        jnp.dot(final_normed, shortlist[0], preferred_element_type=jnp.float32), axis=-1
    )
    learner = jax.nn.log_softmax(student[0], axis=-1)
    picked = (targets[0][:, None] == jnp.arange(student.shape[2])).astype(jnp.float32)
    token_loss = jnp.sum(jnp.exp(teacher) * (teacher - learner), axis=-1) - jnp.sum(
        picked * learner, axis=-1
    )
    counted = jnp.where(decoder, is_valid.astype(jnp.float32), 0.0)
    totals = jnp.stack([jnp.sum(token_loss * counted), jnp.sum(counted)])
    for axis in ("z", "x", "y", "core"):
        totals = lax.psum(totals, axis)
    return (layer_out[None], totals[0] / totals[1])


def solution(mesh):
    segments, expert_devices = mesh.devices.shape
    experts = 4
    fine = Mesh(
        mesh.devices.reshape(segments // 2, 2, experts, expert_devices // experts),
        ("y", "core", "x", "z"),
    )
    seg, exp = (("y", "core"), ("x", "z"))
    placed = (
        P(seg, exp, None),
        P(seg, exp, None),
        P(seg, exp),
        P(seg, exp),
        P(seg, exp, None),
        P(seg, None, None),
        P(seg, None, None),
        P(seg, None, exp),
        P(seg, exp, None),
        P(seg, None, None),
        P(seg, exp, None),
        P(seg, exp),
    )
    return jax.shard_map(
        local, mesh=fine, in_specs=placed, out_specs=(P(seg, exp, None), P()), check_vma=False
    )
```

profile of v0, /device:TPU:1, one launch (start us, length us, event | category | flops | bytes accessed | tf_op | source)
XLA Modules:
  0.0 286.2 jit_solution(16205639869102974398)
XLA Ops:
  7.2 0.0 copy-start
  7.2 0.0 copy-start.1
  7.2 0.0 copy-start.5
  7.2 0.0 all-gather.2.cloned.1.call-start
  7.2 5.8 %collective-permute-start.1 = (bf16[32,2048]{1,0:T(8,128)(2,1)}, bf16[32,2048]{1,0:T(8,128)(2,1)S(1)}, u32[]{:S(2)}, u32[]{:S(2)}) collective-permute-start(bf16[32,2048]{1,0:T(8,128)(2,1)} %bitcast.136), channel_id=1, source_target_pairs={{0,256},{128,384},{1,257},{129,385},{2,258},{130,386},{3,259},{131... | collective-permute-start | bytes 393224 | tf_op jit(solution)/shard_map/ppermute | solution.py:16
  13.7 1.3 collective-permute-start
  15.0 1.0 convert_reduce_fusion
  16.0 0.9 convert_bitcast_fusion
  17.0 0.7 fusion.80
  17.7 1.1 fusion.21
  18.8 0.1 copy.25
  18.9 0.8 slice_bitcast_fusion.1
  20.3 0.1 convolution_add_fusion
  20.5 0.0 collective-permute-done
  20.5 0.0 collective-permute-done.1
  20.5 0.3 fusion.82
  20.8 0.2 fusion.7
  21.1 0.2 copy.20
  21.2 0.2 copy.21
  21.4 1.1 fusion.79
  22.5 1.1 multiply_reduce_fusion
  23.6 0.0 copy-done.1
  23.6 0.0 copy-done.5
  23.6 0.2 fusion.83
  24.0 0.3 convolution_convert_fusion.1
  24.3 10.4 %all_to_all.10 = bf16[4,20,2048]{2,1,0:T(8,128)(2,1)S(1)} all-to-all(bf16[4,20,2048]{2,1,0:T(8,128)(2,1)S(1)} %convolution_convert_fusion.1), channel_id=1, replica_groups=mesh['y'=4,'core'=2,'x'=4,'z'=16] {'x'}, dimensions={0} | all-to-all | bytes 655360 | tf_op jit(solution)/shard_map/all_to_all | solution.py:101
  34.7 0.8 reshape.320
  35.5 0.0 all-gather.2.cloned.1.call-update
  35.5 0.0 reduce-scatter.2.cloned.1.call-start
  35.6 76.6 %all-gather.2.cloned.1.call-done = bf16[1280,2048]{1,0:T(8,128)(2,1)} async-done(((bf16[80,2048]{1,0:T(8,128)(2,1)}), bf16[1280,2048]{1,0:T(8,128)(2,1)}) %all-gather.2.cloned.1.call-update) | async-done | bytes 5242896 | tf_op jit(solution)/shard_map/all_gather | solution.py:102
  112.2 10.8 %convolution_convert_fusion = bf16[1280,2048]{1,0:T(8,128)(2,1)} fusion(bf16[1280,2048]{1,0:T(8,128)(2,1)} %all-gather.2.cloned.1.call-done, bf16[1,256,2048]{2,1,0:T(8,128)(2,1)} %param.21, bf16[1,2048,256]{2,1,0:T(8,128)(2,1)} %param.20), kind=kOutput, calls=%fused_computation.1 | convolution fusion | flops 2687631360 | bytes 12582912 | tf_op jit(solution)/shard_map/dot_general | solution.py:29
  123.0 0.0 copy-start.3
  123.0 0.0 copy-start.4
  123.0 0.0 reduce-scatter.2.cloned.1.call-update
  123.0 76.6 %reduce-scatter.2.cloned.1.call-done = bf16[80,2048]{1,0:T(8,128)(2,1)} async-done(((bf16[1280,2048]{1,0:T(8,128)(2,1)}), bf16[80,2048]{1,0:T(8,128)(2,1)}) %reduce-scatter.2.cloned.1.call-update) | async-done | bytes 327696 | tf_op jit(solution)/shard_map/reduce_scatter | solution.py:106
  199.5 1.8 reshape.321
  201.3 4.0 %all-to-all-start.1 = ((bf16[4,20,2048]{2,1,0:T(8,128)(2,1)}), bf16[4,20,2048]{2,1,0:T(8,128)(2,1)S(1)}, u32[]{:S(2)}, u32[]{:S(2)}) async-start(bf16[4,20,2048]{2,1,0:T(8,128)(2,1)} %reshape.321), calls=%async_computation.2 | async-start | bytes 786432 | tf_op jit(solution)/shard_map/all_to_all | solution.py:107
  205.4 0.0 copy-done.3
  205.4 0.1 bitcast_reduce_fusion
  205.5 0.2 exponential_reduce_fusion
  205.7 5.9 %all-to-all-done.1 = bf16[4,20,2048]{2,1,0:T(8,128)(2,1)S(1)} async-done(((bf16[4,20,2048]{2,1,0:T(8,128)(2,1)}), bf16[4,20,2048]{2,1,0:T(8,128)(2,1)S(1)}, u32[]{:S(2)}, u32[]{:S(2)}) %all-to-all-start.1) | async-done | bytes 327712 | tf_op jit(solution)/shard_map/all_to_all | solution.py:107
  211.6 0.5 convert_reduce_fusion.1
  212.1 0.0 copy-start.2
  212.2 0.2 fusion.17
  212.4 0.0 copy-done
  212.4 0.6 fusion.84
  213.0 0.2 exponential_reduce_fusion.1
  213.2 0.0 copy-done.4
  213.2 0.2 select_reduce_fusion.1
  213.4 0.7 multiply_reduce_fusion.2
  214.1 1.3 pad_maximum_fusion
  215.4 21.9 %psum.28 = f32[2]{0:T(128)S(1)} all-reduce(f32[2]{0:T(128)S(1)} %pad_maximum_fusion), channel_id=1, replica_groups=mesh['y'=4,'core'=2,'x'=4,'z'=16] {'z'}, use_global_device_ids=true, to_apply=%region_19.21 | all-reduce | flops 2 | bytes 16 | tf_op jit(solution)/shard_map/psum | solution.py:129
  237.3 6.6 %psum.29 = f32[2]{0:T(128)S(1)} all-reduce(f32[2]{0:T(128)S(1)} %psum.28), channel_id=1, replica_groups=mesh['y'=4,'core'=2,'x'=4,'z'=16] {'x'}, use_global_device_ids=true, to_apply=%region_20.22 | all-reduce | flops 2 | bytes 16 | tf_op jit(solution)/shard_map/psum | solution.py:129
  243.9 8.3 %psum.30 = f32[2]{0:T(128)S(1)} all-reduce(f32[2]{0:T(128)S(1)} %psum.29), channel_id=1, replica_groups=mesh['y'=4,'core'=2,'x'=4,'z'=16] {'y'}, use_global_device_ids=true, to_apply=%region_21.23 | all-reduce | flops 2 | bytes 16 | tf_op jit(solution)/shard_map/psum | solution.py:129
  252.2 24.1 %psum.31 = f32[2]{0:T(128)S(1)} all-reduce(f32[2]{0:T(128)S(1)} %psum.30), channel_id=1, replica_groups=mesh['y'=4,'core'=2,'x'=4,'z'=16] {'core'}, use_global_device_ids=true, to_apply=%region_22.24 | all-reduce | flops 2 | bytes 16 | tf_op jit(solution)/shard_map/psum | solution.py:129
  276.3 0.6 fusion.81
  278.3 0.0 copy-done.2
  (16 shorter events, 0.1 us)
Async XLA Ops:
  7.2 205.2 %copy-start = (bf16[1,2048,512]{2,1,0:T(8,128)(2,1)S(1)}, bf16[1,2048,512]{2,1,0:T(8,128)(2,1)}, u32[]{:S(2)}) copy-start(bf16[1,2048,512]{2,1,0:T(8,128)(2,1)} %param.22) | copy-start | bytes 6291460
  7.2 16.5 %copy-start.1 = (bf16[1,32,2048]{2,1,0:T(8,128)(2,1)S(1)}, bf16[1,32,2048]{2,1,0:T(8,128)(2,1)}, u32[]{:S(2)}) copy-start(bf16[1,32,2048]{2,1,0:T(8,128)(2,1)} %param.13) | copy-start | bytes 393220
  7.2 16.4 %copy-start.5 = (bf16[1,2048,4]{1,2,0:T(4,128)(2,1)S(1)}, bf16[1,2048,4]{1,2,0:T(4,128)(2,1)}, u32[]{:S(2)}) copy-start(bf16[1,2048,4]{1,2,0:T(4,128)(2,1)} %param.19) | copy-start | bytes 49156
  7.2 105.0 %all-gather.2.cloned.1.call-start = ((), (), s32[]{:S(2)}) async-start(), calls=%async_computation.3 | async-start | bytes 5570560 | tf_op jit(solution)/shard_map/all_gather | solution.py:102
  7.2 13.2 %collective-permute-start.1 = (bf16[32,2048]{1,0:T(8,128)(2,1)}, bf16[32,2048]{1,0:T(8,128)(2,1)S(1)}, u32[]{:S(2)}, u32[]{:S(2)}) collective-permute-start(bf16[32,2048]{1,0:T(8,128)(2,1)} %bitcast.136), channel_id=1, source_target_pairs={{0,256},{128,384},{1,257},{129,385},{2,258},{130,386},{3,259},{131... | collective-permute-start | bytes 393224 | tf_op jit(solution)/shard_map/ppermute | solution.py:16
  13.7 6.8 %collective-permute-start = (bf16[32]{0:T(256)(128)(2,1)S(1)}, bf16[32]{0:T(256)(128)(2,1)S(1)}, u32[]{:S(2)}, u32[]{:S(2)}) collective-permute-start(bf16[32]{0:T(256)(128)(2,1)S(1)} %compare_convert_fusion.1), channel_id=1, source_target_pairs={{0,256},{128,384},{1,257},{129,385},{2,258},{130,386},{3,259},{131... | collective-permute-start | bytes 200 | tf_op jit(solution)/shard_map/ppermute | solution.py:16
  35.5 164.0 %reduce-scatter.2.cloned.1.call-start = ((), (), s32[]{:S(2)}) async-start(), calls=%async_computation.4 | async-start | bytes 5570560 | tf_op jit(solution)/shard_map/reduce_scatter | solution.py:106
  123.0 82.4 %copy-start.3 = (f32[1,32,512]{2,1,0:T(8,128)S(1)}, f32[1,32,512]{2,1,0:T(8,128)}, u32[]{:S(2)}) copy-start(f32[1,32,512]{2,1,0:T(8,128)} %param.23) | copy-start | bytes 196612
  123.0 90.3 %copy-start.4 = (s32[1,32]{1,0:T(1,128)S(1)}, s32[1,32]{1,0:T(1,128)}, u32[]{:S(2)}) copy-start(s32[1,32]{1,0:T(1,128)} %param.24) | copy-start | bytes 388
  201.3 10.3 %all-to-all-start.1 = ((bf16[4,20,2048]{2,1,0:T(8,128)(2,1)}), bf16[4,20,2048]{2,1,0:T(8,128)(2,1)S(1)}, u32[]{:S(2)}, u32[]{:S(2)}) async-start(bf16[4,20,2048]{2,1,0:T(8,128)(2,1)} %reshape.321), calls=%async_computation.2 | async-start | bytes 786432 | tf_op jit(solution)/shard_map/all_to_all | solution.py:107
  212.1 66.1 %copy-start.2 = (bf16[32,2048]{1,0:T(8,128)(2,1)}, bf16[32,2048]{1,0:T(8,128)(2,1)S(1)}, u32[]{:S(2)}) copy-start(bf16[32,2048]{1,0:T(8,128)(2,1)S(1)} %get-tuple-element.21) | copy-start | bytes 393220
Sparse Core Ops, SparseCore 0:
  35.6 76.4 all-gather.1
  123.1 76.3 reduce-scatter.1
where the time goes:
time: 287 us; the launch traced here: 286 us
  waiting for transfers between devices  159 us (55%)
  blocking collectives  71.2 us (25%)
  between operations  18.1 us (6%)
  matrix products  13.2 us (5%)
  starting transfers between devices  11.2 us (4%)
  other arithmetic  8.34 us (3%)
  local copies, waits for them, and re-layouts  5.08 us (2%)
    all_gather x1, waiting for transfers between devices, local(): lax.all_gather(at_expert.reshape(experts * capacity, model_width), 'z', a...  76.6 us
    reduce_scatter x1, waiting for transfers between devices, local(): lax.psum_scatter(partial_out, 'z', scatter_dimension=0, tiled=True)  76.6 us
    psum x4, blocking collectives, local(): totals = lax.psum(totals, axis)  60.9 us
    dot_general x1, matrix products, expert_rows(): jnp.dot(activated, second_weight, preferred_element_type=jnp.float32)  10.8 us
    all_to_all x1, blocking collectives, local(): lax.all_to_all(buffer, 'x', split_axis=0, concat_axis=0, tiled=True)  10.4 us
    ppermute x2, starting transfers between devices, passed_along(): return lax.ppermute(block, axis, route)  7.08 us
    all_to_all x1, waiting for transfers between devices, local(): lax.all_to_all(expert_sum.reshape(experts, capacity, model_width), 'x', s...  5.91 us
  transfers between devices with their start and end apart: 5, of which 3 were waited for; matrix products, arithmetic and copies ran while one was open for 2% of the time, Pallas kernels for 0%

commit v1 on v0

--- a/solution.py
+++ b/solution.py
@@ -99,9 +99,9 @@
         "ect,td->ecd", placing.astype(jnp.bfloat16), normed, preferred_element_type=jnp.float32
     ).astype(jnp.bfloat16)
     at_expert = lax.all_to_all(buffer, "x", split_axis=0, concat_axis=0, tiled=True)
-    rows = lax.all_gather(
-        at_expert.reshape(experts * capacity, model_width), "z", axis=0, tiled=True
-    )
+    own = at_expert.reshape(experts * capacity, model_width)
+    repeated = jnp.stack([own] * lax.axis_size("z"))
+    rows = jnp.concatenate(lax.all_to_all(repeated, "z", 0, 0), axis=0)
     partial_out = expert_rows(rows, w_in[0], w_out[0])
     expert_sum = lax.psum_scatter(partial_out, "z", scatter_dimension=0, tiled=True)
     summed = lax.all_to_all(

time: 287 us -> 445 us (1.55)
  blocking collectives: 71.2 us -> 309 us
  waiting for transfers between devices: 159 us -> 79.2 us
    all_to_all x0 -> x1, blocking collectives: none -> 239 us  [local(): rows = jnp.concatenate(lax.all_to_all(repeated, 'z', 0, 0), axis=0)]
    all_gather x1 -> x0, waiting for transfers between devices: 76.6 us -> none  [local(): lax.all_gather(at_expert.reshape(experts * capacity, model_width), 'z', a...]
  transfers between devices with their start and end apart: 5 -> 4, of which waited for: 3 -> 2; matrix products, arithmetic and copies ran while one was open for 2% -> 1% of each run, Pallas kernels for 0% -> 0%
where the time goes in v1:
time: 445 us; the launch traced here: 444 us
  blocking collectives  309 us (69%)
  waiting for transfers between devices  79.2 us (18%)
  between operations  18.1 us (4%)
  matrix products  13.2 us (3%)
  starting transfers between devices  11.1 us (2%)
  other arithmetic  8.34 us (2%)
  local copies, waits for them, and re-layouts  5.01 us (1%)
    all_to_all x1, blocking collectives, local(): rows = jnp.concatenate(lax.all_to_all(repeated, 'z', 0, 0), axis=0)  239 us
    reduce_scatter x1, waiting for transfers between devices, local(): lax.psum_scatter(partial_out, 'z', scatter_dimension=0, tiled=True)  73.2 us
    psum x4, blocking collectives, local(): totals = lax.psum(totals, axis)  60.4 us
    dot_general x1, matrix products, expert_rows(): jnp.dot(activated, second_weight, preferred_element_type=jnp.float32)  10.7 us
    all_to_all x1, blocking collectives, local(): lax.all_to_all(buffer, 'x', split_axis=0, concat_axis=0, tiled=True)  10.4 us
  transfers between devices with their start and end apart: 4, of which 2 were waited for; matrix products, arithmetic and copies ran while one was open for 1% of the time, Pallas kernels for 0%

profile of v1, /device:TPU:1, one launch (start us, length us, event | category | flops | bytes accessed | tf_op | source)
XLA Modules:
  0.0 444.4 jit_solution(532816589148125224)
XLA Ops:
  7.2 0.0 copy-start
  7.2 0.0 copy-start.1
  7.2 0.0 copy-start.5
  7.2 0.0 reduce-scatter.2.cloned.1.call-start
  7.2 5.8 %collective-permute-start.1 = (bf16[32,2048]{1,0:T(8,128)(2,1)}, bf16[32,2048]{1,0:T(8,128)(2,1)S(1)}, u32[]{:S(2)}, u32[]{:S(2)}) collective-permute-start(bf16[32,2048]{1,0:T(8,128)(2,1)} %bitcast.138), channel_id=1, source_target_pairs={{0,256},{128,384},{1,257},{129,385},{2,258},{130,386},{3,259},{131... | collective-permute-start | bytes 393224 | tf_op jit(solution)/shard_map/ppermute | solution.py:16
  13.7 1.3 collective-permute-start
  15.0 1.0 convert_reduce_fusion
  16.0 0.9 convert_bitcast_fusion
  17.0 0.7 fusion.80
  17.7 1.1 fusion.21
  18.8 0.1 copy.25
  18.9 0.8 slice_bitcast_fusion.1
  20.3 0.1 convolution_add_fusion
  20.5 0.0 collective-permute-done
  20.5 0.0 collective-permute-done.1
  20.5 0.3 fusion.82
  20.8 0.2 fusion.7
  21.1 0.2 copy.20
  21.2 0.2 copy.21
  21.4 1.1 fusion.79
  22.5 1.1 multiply_reduce_fusion
  23.6 0.0 copy-done.1
  23.6 0.0 copy-done.5
  23.6 0.2 fusion.83
  24.0 0.3 convolution_convert_fusion.1
  24.3 10.4 %all_to_all.15 = bf16[4,20,2048]{2,1,0:T(8,128)(2,1)S(1)} all-to-all(bf16[4,20,2048]{2,1,0:T(8,128)(2,1)S(1)} %convolution_convert_fusion.1), channel_id=1, replica_groups=mesh['y'=4,'core'=2,'x'=4,'z'=16] {'x'}, dimensions={0} | all-to-all | bytes 655360 | tf_op jit(solution)/shard_map/all_to_all | solution.py:101
  34.7 0.1 stack_reshape.2
  34.8 0.6 stack.12
  35.4 238.7 %all_to_all.16 = bf16[16,80,2048]{2,1,0:T(8,128)(2,1)} all-to-all(bf16[16,80,2048]{2,1,0:T(8,128)(2,1)S(1)} %stack.12), channel_id=1, replica_groups=mesh['y'=4,'core'=2,'x'=4,'z'=16] {'z'}, dimensions={0} | all-to-all | bytes 10485760 | tf_op jit(solution)/shard_map/all_to_all | solution.py:104
  274.2 10.7 %convolution_convert_fusion = bf16[1280,2048]{1,0:T(8,128)(2,1)} fusion(bf16[1280,2048]{1,0:T(8,128)(2,1)} %bitcast.128, bf16[1,256,2048]{2,1,0:T(8,128)(2,1)} %param.21, bf16[1,2048,256]{2,1,0:T(8,128)(2,1)} %param.20), kind=kOutput, calls=%fused_computation.1 | convolution fusion | flops 2687631360 | bytes 12582912 | tf_op jit(solution)/shard_map/dot_general | solution.py:29
  284.9 0.0 copy-start.3
  284.9 0.0 copy-start.4
  284.9 0.0 reduce-scatter.2.cloned.1.call-update
  284.9 73.2 %reduce-scatter.2.cloned.1.call-done = bf16[80,2048]{1,0:T(8,128)(2,1)} async-done(((bf16[1280,2048]{1,0:T(8,128)(2,1)}), bf16[80,2048]{1,0:T(8,128)(2,1)}) %reduce-scatter.2.cloned.1.call-update) | async-done | bytes 327696 | tf_op jit(solution)/shard_map/reduce_scatter | solution.py:106
  358.2 1.8 reshape.323
  360.0 4.0 all-to-all-start.2
  364.0 0.0 copy-done.3
  364.0 0.1 bitcast_reduce_fusion
  364.1 0.2 exponential_reduce_fusion
  364.3 5.9 %all-to-all-done.2 = bf16[4,20,2048]{2,1,0:T(8,128)(2,1)S(1)} async-done(((bf16[4,20,2048]{2,1,0:T(8,128)(2,1)}), bf16[4,20,2048]{2,1,0:T(8,128)(2,1)S(1)}, u32[]{:S(2)}, u32[]{:S(2)}) %all-to-all-start.2) | async-done | bytes 327712 | tf_op jit(solution)/shard_map/all_to_all | solution.py:107
  370.2 0.5 convert_reduce_fusion.1
  370.7 0.0 copy-start.2
  370.8 0.2 fusion.17
  371.0 0.0 copy-done
  371.0 0.6 fusion.84
  371.6 0.2 exponential_reduce_fusion.1
  371.8 0.0 copy-done.4
  371.8 0.2 select_reduce_fusion.1
  372.0 0.7 multiply_reduce_fusion.2
  372.7 1.3 pad_maximum_fusion
  374.0 21.3 %psum.28 = f32[2]{0:T(128)S(1)} all-reduce(f32[2]{0:T(128)S(1)} %pad_maximum_fusion), channel_id=1, replica_groups=mesh['y'=4,'core'=2,'x'=4,'z'=16] {'z'}, use_global_device_ids=true, to_apply=%region_19.21 | all-reduce | flops 2 | bytes 16 | tf_op jit(solution)/shard_map/psum | solution.py:129
  395.3 6.9 %psum.29 = f32[2]{0:T(128)S(1)} all-reduce(f32[2]{0:T(128)S(1)} %psum.28), channel_id=1, replica_groups=mesh['y'=4,'core'=2,'x'=4,'z'=16] {'x'}, use_global_device_ids=true, to_apply=%region_20.22 | all-reduce | flops 2 | bytes 16 | tf_op jit(solution)/shard_map/psum | solution.py:129
  402.2 8.7 %psum.30 = f32[2]{0:T(128)S(1)} all-reduce(f32[2]{0:T(128)S(1)} %psum.29), channel_id=1, replica_groups=mesh['y'=4,'core'=2,'x'=4,'z'=16] {'y'}, use_global_device_ids=true, to_apply=%region_21.23 | all-reduce | flops 2 | bytes 16 | tf_op jit(solution)/shard_map/psum | solution.py:129
  410.9 23.5 %psum.31 = f32[2]{0:T(128)S(1)} all-reduce(f32[2]{0:T(128)S(1)} %psum.30), channel_id=1, replica_groups=mesh['y'=4,'core'=2,'x'=4,'z'=16] {'core'}, use_global_device_ids=true, to_apply=%region_22.24 | all-reduce | flops 2 | bytes 16 | tf_op jit(solution)/shard_map/psum | solution.py:129
  434.4 0.6 fusion.81
  436.4 0.0 copy-done.2
  (16 shorter events, 0.1 us)
Async XLA Ops:
  7.2 363.8 %copy-start = (bf16[1,2048,512]{2,1,0:T(8,128)(2,1)S(1)}, bf16[1,2048,512]{2,1,0:T(8,128)(2,1)}, u32[]{:S(2)}) copy-start(bf16[1,2048,512]{2,1,0:T(8,128)(2,1)} %param.22) | copy-start | bytes 6291460
  7.2 16.5 %copy-start.1 = (bf16[1,32,2048]{2,1,0:T(8,128)(2,1)S(1)}, bf16[1,32,2048]{2,1,0:T(8,128)(2,1)}, u32[]{:S(2)}) copy-start(bf16[1,32,2048]{2,1,0:T(8,128)(2,1)} %param.13) | copy-start | bytes 393220
  7.2 16.4 %copy-start.5 = (bf16[1,2048,4]{1,2,0:T(4,128)(2,1)S(1)}, bf16[1,2048,4]{1,2,0:T(4,128)(2,1)}, u32[]{:S(2)}) copy-start(bf16[1,2048,4]{1,2,0:T(4,128)(2,1)} %param.19) | copy-start | bytes 49156
  7.2 351.0 %reduce-scatter.2.cloned.1.call-start = ((), (), s32[]{:S(2)}) async-start(), calls=%async_computation.4 | async-start | bytes 5570560 | tf_op jit(solution)/shard_map/reduce_scatter | solution.py:106
  7.2 13.2 %collective-permute-start.1 = (bf16[32,2048]{1,0:T(8,128)(2,1)}, bf16[32,2048]{1,0:T(8,128)(2,1)S(1)}, u32[]{:S(2)}, u32[]{:S(2)}) collective-permute-start(bf16[32,2048]{1,0:T(8,128)(2,1)} %bitcast.138), channel_id=1, source_target_pairs={{0,256},{128,384},{1,257},{129,385},{2,258},{130,386},{3,259},{131... | collective-permute-start | bytes 393224 | tf_op jit(solution)/shard_map/ppermute | solution.py:16
  13.7 6.8 %collective-permute-start = (bf16[32]{0:T(256)(128)(2,1)S(1)}, bf16[32]{0:T(256)(128)(2,1)S(1)}, u32[]{:S(2)}, u32[]{:S(2)}) collective-permute-start(bf16[32]{0:T(256)(128)(2,1)S(1)} %compare_convert_fusion.1), channel_id=1, source_target_pairs={{0,256},{128,384},{1,257},{129,385},{2,258},{130,386},{3,259},{131... | collective-permute-start | bytes 200 | tf_op jit(solution)/shard_map/ppermute | solution.py:16
  284.9 79.0 %copy-start.3 = (f32[1,32,512]{2,1,0:T(8,128)S(1)}, f32[1,32,512]{2,1,0:T(8,128)}, u32[]{:S(2)}) copy-start(f32[1,32,512]{2,1,0:T(8,128)} %param.23) | copy-start | bytes 196612
  284.9 86.9 %copy-start.4 = (s32[1,32]{1,0:T(1,128)S(1)}, s32[1,32]{1,0:T(1,128)}, u32[]{:S(2)}) copy-start(s32[1,32]{1,0:T(1,128)} %param.24) | copy-start | bytes 388
  360.0 10.2 %all-to-all-start.2 = ((bf16[4,20,2048]{2,1,0:T(8,128)(2,1)}), bf16[4,20,2048]{2,1,0:T(8,128)(2,1)S(1)}, u32[]{:S(2)}, u32[]{:S(2)}) async-start(bf16[4,20,2048]{2,1,0:T(8,128)(2,1)} %reshape.323), calls=%async_computation.3 | async-start | bytes 786432 | tf_op jit(solution)/shard_map/all_to_all | solution.py:107
  370.7 65.6 %copy-start.2 = (bf16[32,2048]{1,0:T(8,128)(2,1)}, bf16[32,2048]{1,0:T(8,128)(2,1)S(1)}, u32[]{:S(2)}) copy-start(bf16[32,2048]{1,0:T(8,128)(2,1)S(1)} %get-tuple-element.21) | copy-start | bytes 393220
Sparse Core Ops, SparseCore 0:
  285.1 73.0 reduce-scatter.1
